TPU v7x, 32 devices: a whole 2x2x4 slice. The times are simulated.
32 devices in a mesh: dp: 8 (over y, x, core), mp: 4 (over z).
Axes of the slice: x: 2, y: 2, z: 4, core: 2. Of those that a mesh axis runs over, the one named last changes fastest.
Arguments:
- page_pool: bfloat16 [512, 128, 512], P('dp'), may hold values from -6 to 6
- move_count: int32 [8, 8], P('dp'), may hold values from 0 to 2, as said below
- send_slots: int32 [64, 2], P('dp'), may hold values from 0 to 63, as said below
- page_table: int32 [512, 16], P('dp'), may hold values from 0 to 79, as said below
- history_len: int32 [512], P('dp'), may hold values from 1 to 2048, as said below
- queries: bfloat16 [512, 8, 256], P('dp', 'mp'), may hold values from -6 to 6
- new_entry: bfloat16 [512, 512], P('dp'), may hold values from -6 to 6
- residual: bfloat16 [512, 2048], P('dp'), may hold values from -30 to 30
- out_proj: bfloat16 [2048, 2048], P('mp'), may hold values from -0.125 to 0.125
- ffn_gain: float32 [2048], replicated, may hold values from -0.5 to 0.5
- gate_proj: bfloat16 [2048, 16384], P(None, ('dp', 'mp')), may hold values from -0.125 to 0.125
- up_proj: bfloat16 [2048, 16384], P(None, ('dp', 'mp')), may hold values from -0.125 to 0.125
- down_proj: bfloat16 [16384, 2048], P(('dp', 'mp')), may hold values from -0.046875 to 0.046875
Outputs:
- arrived: bfloat16 [128, 128, 512], P('dp')
- layer_out: bfloat16 [512, 2048], P('dp')
Inputs may be any that keep to these rules, and one draw needn't show every extreme that they name: `move_count`: zero on the diagonal; in every draw one device receives exactly 2 pages from every other device. `send_slots`: only the first move_count[s, d] entries of row s * 8 + d are sent. `page_table`: for a game of device d, an entry e >= 64 equals 64 + s * 2 + c with c < move_count[s, d]. `history_len`: some game of some device reaches 2048 in every draw.
All inputs are finite; a program needn't handle non-finite values.
Results may differ from a plain program's by a relative error of at most 0.0075.
Values may be sent and summed in bfloat16 or wider, within the bound.
A program may use at most 128 MiB of HBM per device.

v0:
```python
import math

import jax
import jax.numpy as jnp
from jax import lax
from jax.sharding import PartitionSpec as P


def attend_block(query_blk, page_rows, length_blk, entry_blk):
    head_size = query_blk.shape[-1]
    keys = page_rows[:, :, :head_size]
    values = page_rows[:, :, head_size:]
    factor = 1.0 / math.sqrt(head_size)
    scores = (
        jnp.einsum("bhd,btd->bht", query_blk, keys, preferred_element_type=jnp.float32) * factor
    )
    own = (
        jnp.einsum(
            "bhd,bd->bh", query_blk, entry_blk[:, :head_size], preferred_element_type=jnp.float32
        )
        * factor
    )
    places = jnp.arange(page_rows.shape[1], dtype=jnp.int32)
    valid = places[None, None, :] < length_blk[:, None, None]
    scores = jnp.where(valid, scores, jnp.float32(-1e30))
    biggest = jnp.maximum(jnp.max(scores, axis=-1), own)
    probs = jnp.where(valid, jnp.exp(scores - biggest[..., None]), jnp.float32(0.0))
    prob_own = jnp.exp(own - biggest)
    denom = jnp.sum(probs, axis=-1) + prob_own
    weights = (probs / denom[..., None]).astype(jnp.bfloat16)
    weight_own = (prob_own / denom).astype(jnp.bfloat16)
    result = jnp.einsum("bht,btd->bhd", weights, values, preferred_element_type=jnp.float32)
    result = result + weight_own.astype(jnp.float32)[..., None] * entry_blk[
        :, None, head_size:
    ].astype(jnp.float32)
    return result.astype(jnp.bfloat16)


def local(
    page_pool,
    move_count,
    send_slots,
    page_table,
    history_len,
    queries,
    new_entry,
    residual,
    out_proj,
    ffn_gain,
    gate_proj,
    up_proj,
    down_proj,
):
    senders = lax.axis_size("dp")
    games = queries.shape[0]
    local_heads = queries.shape[1]
    head_size = queries.shape[2]
    page_len = page_pool.shape[1]
    width = page_pool.shape[2]
    slot_count = send_slots.shape[1]
    table_len = page_table.shape[1]
    live = jnp.arange(slot_count, dtype=jnp.int32)[None, :] < move_count[0][:, None]
    outgoing = page_pool[send_slots]
    outgoing = jnp.where(live[:, :, None, None], outgoing, jnp.zeros((), jnp.bfloat16))
    received = lax.all_to_all(outgoing, "dp", split_axis=0, concat_axis=0, tiled=True)
    arrived = received.reshape(senders * slot_count, page_len, width)
    every_page = jnp.concatenate([page_pool, arrived], axis=0)
    block = math.gcd(games, 8)
    table = page_table.reshape(-1, block, table_len)
    lengths = history_len.reshape(-1, block)
    query_dev = queries.reshape(-1, block, local_heads, head_size)
    entry_dev = new_entry.reshape(-1, block, width)

    def one_block(items):
        table_blk, length_blk, query_blk, entry_blk = items
        page_rows = every_page[table_blk].reshape(block, table_len * page_len, width)
        return attend_block(query_blk, page_rows, length_blk, entry_blk)

    attended = lax.map(one_block, (table, lengths, query_dev, entry_dev)).reshape(
        games, local_heads * head_size
    )
    head_part = jnp.dot(attended, out_proj, preferred_element_type=jnp.float32)
    stream_in = residual.astype(jnp.float32) + lax.psum(head_part, "mp")
    scale_row = lax.rsqrt(jnp.mean(stream_in * stream_in, axis=-1, keepdims=True) + 1e-06)
    normed = (stream_in * scale_row * (1.0 + ffn_gain)).astype(jnp.bfloat16)
    piece = lax.all_gather(normed, "dp", axis=0, tiled=True)
    gate = jnp.dot(piece, gate_proj, preferred_element_type=jnp.float32)
    up_val = jnp.dot(piece, up_proj, preferred_element_type=jnp.float32)
    hidden = (jax.nn.gelu(gate, approximate=True) * up_val).astype(jnp.bfloat16)
    partial_out = lax.psum_scatter(
        jnp.dot(hidden, down_proj, preferred_element_type=jnp.float32),
        "dp",
        scatter_dimension=0,
        tiled=True,
    )
    mixed = lax.psum(partial_out, "mp")
    layer_out = (stream_in + mixed).astype(jnp.bfloat16)
    return (arrived, layer_out)


def solution(mesh):
    in_specs = (
        P("dp", None, None),
        P("dp", None),
        P("dp", None),
        P("dp", None),
        P("dp"),
        P("dp", "mp", None),
        P("dp", None),
        P("dp", None),
        P("mp", None),
        P(),
        P(None, ("dp", "mp")),
        P(None, ("dp", "mp")),
        P(("dp", "mp"), None),
    )
    out_specs = (P("dp", None, None), P("dp", None))
    return jax.shard_map(local, mesh=mesh, in_specs=in_specs, out_specs=out_specs, check_vma=False)
```

profile of v0, /device:TPU:2, one launch (start us, length us, event | category | flops | bytes accessed | tf_op | source)
XLA Modules:
  0.0 444.7 jit_solution(5048033312647142384)
XLA Ops:
  7.2 0.8 compare_select_fusion.1
  8.9 5.4 %gather_fusion.1 = bf16[16,128,512]{2,1,0:T(8,128)(2,1)} fusion(bf16[64,128,512]{2,1,0:T(8,128)(2,1)} %param.15, s32[1024]{0:T(1024)S(1)} %pad_clamp_fusion.1), kind=kCustom, calls=%fused_computation.1 | custom fusion | bytes 4194368 | tf_op jit(solution)/shard_map/gather | solution.py:63
  14.3 3.1 broadcast_select_fusion
  17.4 4.4 all-to-all-start
  22.1 24.9 %all-to-all-done = bf16[8,2,128,512]{3,2,1,0:T(8,128)(2,1)} async-done(((bf16[8,2,128,512]{3,2,1,0:T(8,128)(2,1)}), bf16[8,2,128,512]{3,2,1,0:T(8,128)(2,1)}, u32[]{:S(2)}, u32[]{:S(2)}) %all-to-all-start) | async-done | bytes 2097184 | tf_op jit(solution)/shard_map/all_to_all | solution.py:65
  47.0 11.4 %pad_maximum_fusion = bf16[80,128,512]{2,1,0:T(8,128)(2,1)} fusion(bf16[16,128,512]{2,1,0:T(8,128)(2,1)} %bitcast.11, bf16[64,128,512]{2,1,0:T(8,128)(2,1)} %param.15), kind=kLoop, calls=%fused_computation.35 | loop fusion | flops 5242880 | bytes 20971520 | tf_op jit(solution)/shard_map/concatenate | solution.py:67
  58.5 197.8 %while.10 = (s32[]{:T(128)}, bf16[8,8,2,256]{3,2,1,0:T(2,128)(2,1)S(1)}, s32[8,8]{1,0:T(8,128)S(1)}, bf16[8,8,2,256]{3,2,1,0:T(2,128)(2,1)}, s32[8,8,16]{2,1,0:T...) while((s32[]{:T(128)}, bf16[8,8,2,256]{3,2,1,0:T(2,128)(2,1)S(1)}, ...), condition=%wide.region_3.4_spmd, body=%wide.region_0.3_spmd.sunk | while | flops 33922544 | bytes 50886080 | solution.py:79
  58.6 12.3 %gather_fusion = bf16[128,128,512]{2,1,0:T(8,128)(2,1)} fusion(bf16[80,128,512]{2,1,0:T(8,128)(2,1)} %get-tuple-element.136, s32[1024]{0:T(1024)S(1)} %pad_clamp_fusion.3), kind=kCustom, calls=%fused_computation.clone.1 | custom fusion | bytes 33554944 | tf_op jit(solution)/shard_map/while/body/eval_jaxpr/gather | solution.py:76
  71.0 5.8 %fusion.71 = (f32[8,2]{1,0:T(8,128)S(1)}, f32[8,2,2048]{2,1,0:T(2,128)S(1)}) fusion(bf16[8,2048,512]{2,1,0:T(8,128)(2,1)} %bitcast.55, bf16[8,8,2,256]{3,2,1,0:T(2,128)(2,1)} %get-tuple-element.134, s32[]{:T(128)} %get-tuple-element.123, pred[8,2048]{1,0:T(8,128)(4,1)S(1)} %iota_compare_fusion.3), kind=kOutput, calls=%fused_computation.65.clone.1 | convolution fusion | flops 16875504 | bytes 8544832 | tf_op jit(solution)/shard_map/while/body/eval_jaxpr/bhd,btd->bht/dot_general | solution.py:15
  77.4 0.8 fusion.69
  78.6 4.6 %fusion.74 = bf16[8,8,2,256]{3,2,1,0:T(2,128)(2,1)S(1)} fusion(bf16[8,8,2,256]{3,2,1,0:T(2,128)(2,1)S(1)} %get-tuple-element.124, s32[]{:T(128)} %get-tuple-element.123, bf16[8,2048,512]{2,1,0:T(8,128)(2,1)} %bitcast.56, f32[8,2]{1,0:T(8,128)S(1)} %get-tuple-element.112, f32[8,2,2048]{2,1,0:T(2,128)S(1)} %get-tuple-element.110, ...), kind=kOutput, calls=%fused_computation.11.clone.1 | convolution fusion | flops 16920576 | bytes 8565248 | tf_op jit(solution)/shard_map/while/body/eval_jaxpr/bht,btd->bhd/dot_general | solution.py:32
  83.3 12.3 %gather_fusion = bf16[128,128,512]{2,1,0:T(8,128)(2,1)} fusion(bf16[80,128,512]{2,1,0:T(8,128)(2,1)} %get-tuple-element.136, s32[1024]{0:T(1024)S(1)} %pad_clamp_fusion.3), kind=kCustom, calls=%fused_computation.clone.1 | custom fusion | bytes 33554944 | tf_op jit(solution)/shard_map/while/body/eval_jaxpr/gather | solution.py:76
  95.7 5.8 %fusion.71 = (f32[8,2]{1,0:T(8,128)S(1)}, f32[8,2,2048]{2,1,0:T(2,128)S(1)}) fusion(bf16[8,2048,512]{2,1,0:T(8,128)(2,1)} %bitcast.55, bf16[8,8,2,256]{3,2,1,0:T(2,128)(2,1)} %get-tuple-element.134, s32[]{:T(128)} %get-tuple-element.123, pred[8,2048]{1,0:T(8,128)(4,1)S(1)} %iota_compare_fusion.3), kind=kOutput, calls=%fused_computation.65.clone.1 | convolution fusion | flops 16875504 | bytes 8544832 | tf_op jit(solution)/shard_map/while/body/eval_jaxpr/bhd,btd->bht/dot_general | solution.py:15
  102.1 0.8 fusion.69
  103.3 4.6 %fusion.74 = bf16[8,8,2,256]{3,2,1,0:T(2,128)(2,1)S(1)} fusion(bf16[8,8,2,256]{3,2,1,0:T(2,128)(2,1)S(1)} %get-tuple-element.124, s32[]{:T(128)} %get-tuple-element.123, bf16[8,2048,512]{2,1,0:T(8,128)(2,1)} %bitcast.56, f32[8,2]{1,0:T(8,128)S(1)} %get-tuple-element.112, f32[8,2,2048]{2,1,0:T(2,128)S(1)} %get-tuple-element.110, ...), kind=kOutput, calls=%fused_computation.11.clone.1 | convolution fusion | flops 16920576 | bytes 8565248 | tf_op jit(solution)/shard_map/while/body/eval_jaxpr/bht,btd->bhd/dot_general | solution.py:32
  108.0 12.3 %gather_fusion = bf16[128,128,512]{2,1,0:T(8,128)(2,1)} fusion(bf16[80,128,512]{2,1,0:T(8,128)(2,1)} %get-tuple-element.136, s32[1024]{0:T(1024)S(1)} %pad_clamp_fusion.3), kind=kCustom, calls=%fused_computation.clone.1 | custom fusion | bytes 33554944 | tf_op jit(solution)/shard_map/while/body/eval_jaxpr/gather | solution.py:76
  120.4 5.8 %fusion.71 = (f32[8,2]{1,0:T(8,128)S(1)}, f32[8,2,2048]{2,1,0:T(2,128)S(1)}) fusion(bf16[8,2048,512]{2,1,0:T(8,128)(2,1)} %bitcast.55, bf16[8,8,2,256]{3,2,1,0:T(2,128)(2,1)} %get-tuple-element.134, s32[]{:T(128)} %get-tuple-element.123, pred[8,2048]{1,0:T(8,128)(4,1)S(1)} %iota_compare_fusion.3), kind=kOutput, calls=%fused_computation.65.clone.1 | convolution fusion | flops 16875504 | bytes 8544832 | tf_op jit(solution)/shard_map/while/body/eval_jaxpr/bhd,btd->bht/dot_general | solution.py:15
  126.9 0.8 fusion.69
  128.0 4.6 %fusion.74 = bf16[8,8,2,256]{3,2,1,0:T(2,128)(2,1)S(1)} fusion(bf16[8,8,2,256]{3,2,1,0:T(2,128)(2,1)S(1)} %get-tuple-element.124, s32[]{:T(128)} %get-tuple-element.123, bf16[8,2048,512]{2,1,0:T(8,128)(2,1)} %bitcast.56, f32[8,2]{1,0:T(8,128)S(1)} %get-tuple-element.112, f32[8,2,2048]{2,1,0:T(2,128)S(1)} %get-tuple-element.110, ...), kind=kOutput, calls=%fused_computation.11.clone.1 | convolution fusion | flops 16920576 | bytes 8565248 | tf_op jit(solution)/shard_map/while/body/eval_jaxpr/bht,btd->bhd/dot_general | solution.py:32
  132.7 12.3 %gather_fusion = bf16[128,128,512]{2,1,0:T(8,128)(2,1)} fusion(bf16[80,128,512]{2,1,0:T(8,128)(2,1)} %get-tuple-element.136, s32[1024]{0:T(1024)S(1)} %pad_clamp_fusion.3), kind=kCustom, calls=%fused_computation.clone.1 | custom fusion | bytes 33554944 | tf_op jit(solution)/shard_map/while/body/eval_jaxpr/gather | solution.py:76
  145.1 5.8 %fusion.71 = (f32[8,2]{1,0:T(8,128)S(1)}, f32[8,2,2048]{2,1,0:T(2,128)S(1)}) fusion(bf16[8,2048,512]{2,1,0:T(8,128)(2,1)} %bitcast.55, bf16[8,8,2,256]{3,2,1,0:T(2,128)(2,1)} %get-tuple-element.134, s32[]{:T(128)} %get-tuple-element.123, pred[8,2048]{1,0:T(8,128)(4,1)S(1)} %iota_compare_fusion.3), kind=kOutput, calls=%fused_computation.65.clone.1 | convolution fusion | flops 16875504 | bytes 8544832 | tf_op jit(solution)/shard_map/while/body/eval_jaxpr/bhd,btd->bht/dot_general | solution.py:15
  151.6 0.8 fusion.69
  152.7 4.6 %fusion.74 = bf16[8,8,2,256]{3,2,1,0:T(2,128)(2,1)S(1)} fusion(bf16[8,8,2,256]{3,2,1,0:T(2,128)(2,1)S(1)} %get-tuple-element.124, s32[]{:T(128)} %get-tuple-element.123, bf16[8,2048,512]{2,1,0:T(8,128)(2,1)} %bitcast.56, f32[8,2]{1,0:T(8,128)S(1)} %get-tuple-element.112, f32[8,2,2048]{2,1,0:T(2,128)S(1)} %get-tuple-element.110, ...), kind=kOutput, calls=%fused_computation.11.clone.1 | convolution fusion | flops 16920576 | bytes 8565248 | tf_op jit(solution)/shard_map/while/body/eval_jaxpr/bht,btd->bhd/dot_general | solution.py:32
  157.4 12.3 %gather_fusion = bf16[128,128,512]{2,1,0:T(8,128)(2,1)} fusion(bf16[80,128,512]{2,1,0:T(8,128)(2,1)} %get-tuple-element.136, s32[1024]{0:T(1024)S(1)} %pad_clamp_fusion.3), kind=kCustom, calls=%fused_computation.clone.1 | custom fusion | bytes 33554944 | tf_op jit(solution)/shard_map/while/body/eval_jaxpr/gather | solution.py:76
  169.8 5.8 %fusion.71 = (f32[8,2]{1,0:T(8,128)S(1)}, f32[8,2,2048]{2,1,0:T(2,128)S(1)}) fusion(bf16[8,2048,512]{2,1,0:T(8,128)(2,1)} %bitcast.55, bf16[8,8,2,256]{3,2,1,0:T(2,128)(2,1)} %get-tuple-element.134, s32[]{:T(128)} %get-tuple-element.123, pred[8,2048]{1,0:T(8,128)(4,1)S(1)} %iota_compare_fusion.3), kind=kOutput, calls=%fused_computation.65.clone.1 | convolution fusion | flops 16875504 | bytes 8544832 | tf_op jit(solution)/shard_map/while/body/eval_jaxpr/bhd,btd->bht/dot_general | solution.py:15
  176.3 0.8 fusion.69
  177.4 4.6 %fusion.74 = bf16[8,8,2,256]{3,2,1,0:T(2,128)(2,1)S(1)} fusion(bf16[8,8,2,256]{3,2,1,0:T(2,128)(2,1)S(1)} %get-tuple-element.124, s32[]{:T(128)} %get-tuple-element.123, bf16[8,2048,512]{2,1,0:T(8,128)(2,1)} %bitcast.56, f32[8,2]{1,0:T(8,128)S(1)} %get-tuple-element.112, f32[8,2,2048]{2,1,0:T(2,128)S(1)} %get-tuple-element.110, ...), kind=kOutput, calls=%fused_computation.11.clone.1 | convolution fusion | flops 16920576 | bytes 8565248 | tf_op jit(solution)/shard_map/while/body/eval_jaxpr/bht,btd->bhd/dot_general | solution.py:32
  182.2 12.3 %gather_fusion = bf16[128,128,512]{2,1,0:T(8,128)(2,1)} fusion(bf16[80,128,512]{2,1,0:T(8,128)(2,1)} %get-tuple-element.136, s32[1024]{0:T(1024)S(1)} %pad_clamp_fusion.3), kind=kCustom, calls=%fused_computation.clone.1 | custom fusion | bytes 33554944 | tf_op jit(solution)/shard_map/while/body/eval_jaxpr/gather | solution.py:76
  194.5 5.8 %fusion.71 = (f32[8,2]{1,0:T(8,128)S(1)}, f32[8,2,2048]{2,1,0:T(2,128)S(1)}) fusion(bf16[8,2048,512]{2,1,0:T(8,128)(2,1)} %bitcast.55, bf16[8,8,2,256]{3,2,1,0:T(2,128)(2,1)} %get-tuple-element.134, s32[]{:T(128)} %get-tuple-element.123, pred[8,2048]{1,0:T(8,128)(4,1)S(1)} %iota_compare_fusion.3), kind=kOutput, calls=%fused_computation.65.clone.1 | convolution fusion | flops 16875504 | bytes 8544832 | tf_op jit(solution)/shard_map/while/body/eval_jaxpr/bhd,btd->bht/dot_general | solution.py:15
  202.1 4.6 %fusion.74 = bf16[8,8,2,256]{3,2,1,0:T(2,128)(2,1)S(1)} fusion(bf16[8,8,2,256]{3,2,1,0:T(2,128)(2,1)S(1)} %get-tuple-element.124, s32[]{:T(128)} %get-tuple-element.123, bf16[8,2048,512]{2,1,0:T(8,128)(2,1)} %bitcast.56, f32[8,2]{1,0:T(8,128)S(1)} %get-tuple-element.112, f32[8,2,2048]{2,1,0:T(2,128)S(1)} %get-tuple-element.110, ...), kind=kOutput, calls=%fused_computation.11.clone.1 | convolution fusion | flops 16920576 | bytes 8565248 | tf_op jit(solution)/shard_map/while/body/eval_jaxpr/bht,btd->bhd/dot_general | solution.py:32
  206.9 12.3 %gather_fusion = bf16[128,128,512]{2,1,0:T(8,128)(2,1)} fusion(bf16[80,128,512]{2,1,0:T(8,128)(2,1)} %get-tuple-element.136, s32[1024]{0:T(1024)S(1)} %pad_clamp_fusion.3), kind=kCustom, calls=%fused_computation.clone.1 | custom fusion | bytes 33554944 | tf_op jit(solution)/shard_map/while/body/eval_jaxpr/gather | solution.py:76
  219.3 5.8 %fusion.71 = (f32[8,2]{1,0:T(8,128)S(1)}, f32[8,2,2048]{2,1,0:T(2,128)S(1)}) fusion(bf16[8,2048,512]{2,1,0:T(8,128)(2,1)} %bitcast.55, bf16[8,8,2,256]{3,2,1,0:T(2,128)(2,1)} %get-tuple-element.134, s32[]{:T(128)} %get-tuple-element.123, pred[8,2048]{1,0:T(8,128)(4,1)S(1)} %iota_compare_fusion.3), kind=kOutput, calls=%fused_computation.65.clone.1 | convolution fusion | flops 16875504 | bytes 8544832 | tf_op jit(solution)/shard_map/while/body/eval_jaxpr/bhd,btd->bht/dot_general | solution.py:15
  225.7 0.8 fusion.69
  226.9 4.6 %fusion.74 = bf16[8,8,2,256]{3,2,1,0:T(2,128)(2,1)S(1)} fusion(bf16[8,8,2,256]{3,2,1,0:T(2,128)(2,1)S(1)} %get-tuple-element.124, s32[]{:T(128)} %get-tuple-element.123, bf16[8,2048,512]{2,1,0:T(8,128)(2,1)} %bitcast.56, f32[8,2]{1,0:T(8,128)S(1)} %get-tuple-element.112, f32[8,2,2048]{2,1,0:T(2,128)S(1)} %get-tuple-element.110, ...), kind=kOutput, calls=%fused_computation.11.clone.1 | convolution fusion | flops 16920576 | bytes 8565248 | tf_op jit(solution)/shard_map/while/body/eval_jaxpr/bht,btd->bhd/dot_general | solution.py:32
  231.6 12.3 %gather_fusion = bf16[128,128,512]{2,1,0:T(8,128)(2,1)} fusion(bf16[80,128,512]{2,1,0:T(8,128)(2,1)} %get-tuple-element.136, s32[1024]{0:T(1024)S(1)} %pad_clamp_fusion.3), kind=kCustom, calls=%fused_computation.clone.1 | custom fusion | bytes 33554944 | tf_op jit(solution)/shard_map/while/body/eval_jaxpr/gather | solution.py:76
  244.0 5.8 %fusion.71 = (f32[8,2]{1,0:T(8,128)S(1)}, f32[8,2,2048]{2,1,0:T(2,128)S(1)}) fusion(bf16[8,2048,512]{2,1,0:T(8,128)(2,1)} %bitcast.55, bf16[8,8,2,256]{3,2,1,0:T(2,128)(2,1)} %get-tuple-element.134, s32[]{:T(128)} %get-tuple-element.123, pred[8,2048]{1,0:T(8,128)(4,1)S(1)} %iota_compare_fusion.3), kind=kOutput, calls=%fused_computation.65.clone.1 | convolution fusion | flops 16875504 | bytes 8544832 | tf_op jit(solution)/shard_map/while/body/eval_jaxpr/bhd,btd->bht/dot_general | solution.py:15
  251.6 4.6 %fusion.74 = bf16[8,8,2,256]{3,2,1,0:T(2,128)(2,1)S(1)} fusion(bf16[8,8,2,256]{3,2,1,0:T(2,128)(2,1)S(1)} %get-tuple-element.124, s32[]{:T(128)} %get-tuple-element.123, bf16[8,2048,512]{2,1,0:T(8,128)(2,1)} %bitcast.56, f32[8,2]{1,0:T(8,128)S(1)} %get-tuple-element.112, f32[8,2,2048]{2,1,0:T(2,128)S(1)} %get-tuple-element.110, ...), kind=kOutput, calls=%fused_computation.11.clone.1 | convolution fusion | flops 16920576 | bytes 8565248 | tf_op jit(solution)/shard_map/while/body/eval_jaxpr/bht,btd->bhd/dot_general | solution.py:32
  256.3 2.9 fusion.50
  259.3 39.3 %all-reduce.3.cloned.1.call-done = f32[64,2048]{1,0:T(8,128)} async-done(((f32[64,2048]{1,0:T(8,128)}), f32[64,2048]{1,0:T(8,128)}) %all-reduce.3.cloned.1.call-update) | async-done | bytes 524304 | tf_op jit(solution)/shard_map/psum | solution.py:83
  298.6 1.2 multiply_reduce_fusion
  299.8 1.9 multiply_convert_fusion
  301.8 28.0 %all-gather.2.cloned.1.call-done = bf16[512,2048]{1,0:T(8,128)(2,1)} async-done(((bf16[64,2048]{1,0:T(8,128)(2,1)}), bf16[512,2048]{1,0:T(8,128)(2,1)}) %all-gather.2.cloned.1.call-update) | async-done | bytes 2097168 | tf_op jit(solution)/shard_map/all_gather | solution.py:86
  329.7 4.4 fusion.51
  334.2 6.9 %fusion.40 = f32[512,2048]{1,0:T(8,128)} fusion(bf16[512,2048]{1,0:T(8,128)(2,1)S(1)} %copy-done, bf16[512,2048]{1,0:T(8,128)(2,1)} %all-gather.2.cloned.1.call-done, bf16[2048,512]{1,0:T(8,128)(2,1)} %param.26, f32[512,512]{1,0:T(8,128)} %fusion.51), kind=kOutput, calls=%fused_computation.47 | convolution fusion | flops 2150105088 | bytes 11534336 | tf_op jit(solution)/shard_map/dot_general | solution.py:91
  341.2 51.4 %reduce-scatter.2.cloned.1.call-done = f32[64,2048]{1,0:T(8,128)} async-done(((f32[512,2048]{1,0:T(8,128)}), f32[64,2048]{1,0:T(8,128)}) %reduce-scatter.2.cloned.1.call-update) | async-done | bytes 524304 | tf_op jit(solution)/shard_map/reduce_scatter | solution.py:90
  392.6 40.7 %all-reduce.5.cloned.1.call-done = f32[64,2048]{1,0:T(8,128)} async-done(((f32[64,2048]{1,0:T(8,128)}), f32[64,2048]{1,0:T(8,128)}) %all-reduce.5.cloned.1.call-update) | async-done | bytes 524304 | tf_op jit(solution)/shard_map/psum | solution.py:96
  433.3 1.8 add_convert_fusion
  435.1 3.1 copy.38
  (112 shorter events, 12.6 us)
Async XLA Ops:
  7.2 327.0 %copy-start = (bf16[512,2048]{1,0:T(8,128)(2,1)S(1)}, bf16[512,2048]{1,0:T(8,128)(2,1)}, u32[]{:S(2)}) copy-start(bf16[512,2048]{1,0:T(8,128)(2,1)} %param.27) | copy-start | bytes 6291460
  17.4 4.5 %copy-start.3 = (s32[64,16]{0,1:T(8,128)S(1)}, s32[64,16]{0,1:T(8,128)}, u32[]{:S(2)}) copy-start(s32[64,16]{0,1:T(8,128)} %param.18) | copy-start | bytes 12292
  17.4 4.6 %copy-start.5 = (s32[64]{0:T(128)S(1)}, s32[64]{0:T(128)}, u32[]{:S(2)}) copy-start(s32[64]{0:T(128)} %param.19) | copy-start | bytes 772
  17.4 29.6 %all-to-all-start = ((bf16[8,2,128,512]{3,2,1,0:T(8,128)(2,1)}), bf16[8,2,128,512]{3,2,1,0:T(8,128)(2,1)}, u32[]{:S(2)}, u32[]{:S(2)}) async-start(bf16[8,2,128,512]{3,2,1,0:T(8,128)(2,1)} %broadcast_select_fusion), calls=%async_computation | async-start | bytes 4194304 | tf_op jit(solution)/shard_map/all_to_all | solution.py:65
  21.9 276.7 %all-reduce.3.cloned.1.call-start = ((), (), s32[]{:S(2)}) async-start(), calls=%async_computation.2 | async-start | bytes 1048576 | tf_op jit(solution)/shard_map/psum | solution.py:83
  256.2 3.0 copy-start.4
  256.3 42.3 %copy-start.2 = (bf16[64,2048]{1,0:T(8,128)(2,1)S(1)}, bf16[64,2048]{1,0:T(8,128)(2,1)}, u32[]{:S(2)}) copy-start(bf16[64,2048]{1,0:T(8,128)(2,1)} %param.22) | copy-start | bytes 786436
  259.2 70.5 %all-gather.2.cloned.1.call-start = ((), (), s32[]{:S(2)}) async-start(), calls=%async_computation.3 | async-start | bytes 2359296 | tf_op jit(solution)/shard_map/all_gather | solution.py:86
  301.7 90.9 %reduce-scatter.2.cloned.1.call-start = ((), (), s32[]{:S(2)}) async-start(), calls=%async_computation.4 | async-start | bytes 4718592 | tf_op jit(solution)/shard_map/reduce_scatter | solution.py:90
  341.1 92.2 %copy-start.1 = (f32[64,2048]{1,0:T(8,128)S(1)}, f32[64,2048]{1,0:T(8,128)}, u32[]{:S(2)}) copy-start(f32[64,2048]{1,0:T(8,128)} %all-reduce.3.cloned.1.call-done) | copy-start | bytes 1572868
  341.1 92.2 %all-reduce.5.cloned.1.call-start = ((), (), s32[]{:S(2)}) async-start(), calls=%async_computation.5 | async-start | bytes 1048576 | tf_op jit(solution)/shard_map/psum | solution.py:96
Sparse Core Ops, SparseCore 0:
  259.3 39.1 all-reduce.2
  301.8 27.8 all-gather.1
  341.3 51.2 reduce-scatter.1
  394.9 38.3 all-reduce.4
where the time goes:
time: 448 us; the launch traced here: 445 us
  waiting for transfers between devices  184 us (41%)
  local copies, waits for them, and re-layouts  114 us (25%)
  matrix products  104 us (23%)
  other arithmetic  24.3 us (5%)
  between operations  13.9 us (3%)
  starting transfers between devices  4.61 us (1%)
    gather x8, local copies, waits for them, and re-layouts, one_block(): every_page[table_blk].reshape(block, table_len * page_len, width)  98.3 us
    reduce_scatter x1, waiting for transfers between devices, local(): lax.psum_scatter(jnp.dot(hidden, down_proj, preferred_element_type=jnp.fl...  51.4 us
    dot_general x8, matrix products, attend_block(): jnp.einsum('bhd,btd->bht', query_blk, keys, preferred_element_type=jnp.fl...  46 us
    psum x1, waiting for transfers between devices, local(): mixed = lax.psum(partial_out, 'mp')  40.7 us
    psum x1, waiting for transfers between devices, local(): stream_in = residual.astype(jnp.float32) + lax.psum(head_part, 'mp')  39.3 us
    dot_general x8, matrix products, attend_block(): jnp.einsum('bht,btd->bhd', weights, values, preferred_element_type=jnp.fl...  37.1 us
    all_gather x1, waiting for transfers between devices, local(): piece = lax.all_gather(normed, 'dp', axis=0, tiled=True)  28 us
    all_to_all x1, waiting for transfers between devices, local(): lax.all_to_all(outgoing, 'dp', split_axis=0, concat_axis=0, tiled=True)  24.9 us
  transfers between devices with their start and end apart: 5, of which 5 were waited for; matrix products, arithmetic and copies ran while one was open for 0% of the time, Pallas kernels for 0%

commit v1 on v0

v1 whole, which is shorter than its diff:
```python
import functools
import math

import jax
import jax.numpy as jnp
from jax import lax
from jax.experimental import pallas as pl
from jax.experimental.pallas import tpu as pltpu
from jax.sharding import PartitionSpec as P

F32 = jnp.float32
BF16 = jnp.bfloat16


def remote(src, dst, send, recv, axis, peer):
    return pltpu.make_async_remote_copy(
        src_ref=src,
        dst_ref=dst,
        send_sem=send,
        recv_sem=recv,
        device_id={axis: peer},
        device_id_type=pl.DeviceIdType.MESH,
    )


def flip(index, bit):
    size = 1 << bit
    return index + size * (1 - 2 * ((index // size) % 2))


def flips(index, bits):
    found = [index]
    for bit in bits:
        found = found + [flip(f, bit) for f in found]
    return found


def with_bits(index, bits, number):
    for place, bit in enumerate(bits):
        size = 1 << bit
        index = index + size * (((number >> place) & 1) - (index // size) % 2)
    return index


def dot(a, b):
    return jnp.dot(a, b, preferred_element_type=F32)


def step(
    n_dp,
    n_mp,
    count_ref,
    slot_ref,
    table_ref,
    length_ref,
    query_ref,
    entry_ref,
    residual_ref,
    gain_ref,
    pool_hbm,
    wo_hbm,
    wg_hbm,
    wu_hbm,
    wd_hbm,
    arrived_hbm,
    out_ref,
    pages,
    landed,
    outgoing,
    wo,
    wg,
    wu,
    wd,
    head32,
    head16,
    sums16,
    head_got,
    sums_got,
    feats,
    hidden,
    part,
    got,
    pool_sem,
    weight_sem,
    arrived_sem,
    page_send,
    page_recv,
    z_send,
    z_recv,
    ag_send,
    ag_recv,
    rs_send,
    rs_recv,
):
    dp = lax.axis_index("dp")
    mp = lax.axis_index("mp")
    bits = n_dp.bit_length() - 1
    pool, page_len, width = pool_hbm.shape
    cap = slot_ref.shape[1]
    games, table_len = table_ref.shape
    rows, head_size = query_ref.shape
    heads = rows // games
    model = residual_ref.shape[1]
    half = model // 2
    share = games // n_mp
    every = pool + n_dp * cap
    group = math.gcd(pool, n_dp * cap, 8)
    pool_loads = []
    for at in range(0, pool, group):
        copy = pltpu.make_async_copy(
            pool_hbm.at[pl.ds(at, group)], pages.at[pl.ds(at, group)], pool_sem.at[at // group]
        )
        copy.start()
        pool_loads.append(copy)
    weight_loads = []
    for i, (src, dst) in enumerate(((wo_hbm, wo), (wg_hbm, wg), (wu_hbm, wu), (wd_hbm, wd))):
        copy = pltpu.make_async_copy(src, dst, weight_sem.at[i])
        copy.start()
        weight_loads.append(copy)

    barrier = pltpu.get_barrier_semaphore()
    for axis, n, me in (("dp", n_dp, dp), ("mp", n_mp, mp)):
        for o in range(1, n):
            pl.semaphore_signal(
                barrier,
                inc=1,
                device_id={axis: lax.rem(me + o, n)},
                device_id_type=pl.DeviceIdType.MESH,
            )
    for copy in pool_loads:
        copy.wait()
    for d in range(n_dp):
        for c in range(cap):
            page = pages[slot_ref[d, c]]
            live = jnp.full(page.shape, c < count_ref[0, d])
            outgoing[d * cap + c] = jnp.where(live, page, jnp.zeros_like(page))
    pl.semaphore_wait(barrier, n_dp - 1 + n_mp - 1)

    sends = []
    for o in range(1, n_dp):
        to = lax.rem(dp + o, n_dp)
        copy = remote(
            outgoing.at[pl.ds(to * cap, cap)],
            landed.at[pl.ds(dp * cap, cap)],
            page_send.at[o - 1],
            page_recv.at[o - 1],
            "dp",
            to,
        )
        copy.start()
        sends.append(copy)
    landed[pl.ds(dp * cap, cap)] = outgoing[pl.ds(dp * cap, cap)]

    table = table_ref[...]
    length = length_ref[...]
    whole_pages = lax.div(length, jnp.int32(page_len))
    rest = length - whole_pages * page_len
    lane = lax.broadcasted_iota(jnp.int32, (games, every), 1)
    full = jnp.zeros((games, every), F32)
    last = jnp.full((games, 1), -1, jnp.int32)
    for j in range(table_len):
        named = table[:, j : j + 1]
        full = full + jnp.where((lane == named) & (whole_pages > j), 1.0, 0.0)
        last = jnp.where(whole_pages == j, named, last)
    full = jnp.concatenate([full] * heads, axis=0)
    last = jnp.concatenate([last] * heads, axis=0)
    rest = jnp.concatenate([rest] * heads, axis=0)
    place = lax.broadcasted_iota(jnp.int32, (rows, page_len), 1)
    in_last = jnp.where(place < rest, 1.0, 0.0)

    factor = 1.0 / math.sqrt(head_size)
    query = query_ref[...]
    entry = entry_ref[...].astype(F32)
    entry = jnp.concatenate([entry] * heads, axis=0)
    biggest = (
        jnp.sum(query.astype(F32) * entry[:, :head_size], axis=-1, keepdims=True) * factor
    )
    total = jnp.ones((rows, 1), F32)
    acc = entry[:, head_size:]

    def attend(at, state):
        biggest, total, acc = state
        block = pages.at[pl.ds(at, group)] if at < pool else landed.at[pl.ds(at - pool, group)]
        keys = block[:, :, :head_size].reshape(group * page_len, head_size)
        values = block[:, :, head_size:].reshape(group * page_len, head_size)
        scores = (
            lax.dot_general(query, keys, (((1,), (1,)), ((), ())), preferred_element_type=F32)
            * factor
        )
        times = jnp.concatenate(
            [
                full[:, e : e + 1] + jnp.where(last == e, in_last, 0.0)
                for e in range(at, at + group)
            ],
            axis=1,
        )
        scores = jnp.where(times > 0.0, scores, -1e30)
        new = jnp.maximum(biggest, jnp.max(scores, axis=-1, keepdims=True))
        probs = times * jnp.exp(scores - new)
        shrink = jnp.exp(biggest - new)
        total = total * shrink + jnp.sum(probs, axis=-1, keepdims=True)
        acc = acc * shrink + dot(probs.astype(BF16), values)
        return new, total, acc

    state = (biggest, total, acc)
    for at in range(0, pool, group):
        state = attend(at, state)
    for o in range(1, n_dp):
        source = lax.rem(dp - o + n_dp, n_dp)
        slot = landed.at[pl.ds(source * cap, cap)]
        remote(slot, slot, page_send.at[o - 1], page_recv.at[o - 1], "dp", source).wait_recv()
    arrived_copy = pltpu.make_async_copy(landed, arrived_hbm, arrived_sem)
    arrived_copy.start()
    for at in range(pool, every, group):
        state = attend(at, state)
    biggest, total, acc = state
    attended = (acc / total).astype(BF16)
    attended = jnp.concatenate(
        [attended[h * games : (h + 1) * games] for h in range(heads)], axis=1
    )
    weight_loads[0].wait()
    head = dot(attended, wo[...])
    head32[...] = head
    head16[...] = head.astype(BF16)

    def sum_mp(block, landing, base):
        for o in range(1, n_mp):
            to = lax.rem(mp + o, n_mp)
            copy = remote(
                block.at[pl.ds(pl.multiple_of(to * share, share), share)],
                landing.at[o - 1],
                z_send.at[base + o - 1],
                z_recv.at[base + o - 1],
                "mp",
                to,
            )
            copy.start()
            sends.append(copy)
        total = head32[pl.ds(pl.multiple_of(mp * share, share), share)]
        for o in range(1, n_mp):
            remote(
                landing.at[o - 1],
                landing.at[o - 1],
                z_send.at[base + o - 1],
                z_recv.at[base + o - 1],
                "mp",
                lax.rem(mp - o + n_mp, n_mp),
            ).wait_recv()
            total = total + landing[o - 1].astype(F32)
        return total

    def spread_mp(views, base):
        per = len(views(mp))
        for o in range(1, n_mp):
            for i, view in enumerate(views(mp)):
                sem = base + (o - 1) * per + i
                copy = remote(
                    view, view, z_send.at[sem], z_recv.at[sem], "mp", lax.rem(mp + o, n_mp)
                )
                copy.start()
                sends.append(copy)
        for o in range(1, n_mp):
            source = lax.rem(mp - o + n_mp, n_mp)
            for i, view in enumerate(views(source)):
                sem = base + (o - 1) * per + i
                remote(view, view, z_send.at[sem], z_recv.at[sem], "mp", source).wait_recv()

    def own_rows(m):
        return pl.ds(pl.multiple_of(m * share, share), share)

    peers = n_mp - 1
    mine = residual_ref[own_rows(mp)].astype(F32) + sum_mp(head16, head_got, 0)
    scale = lax.rsqrt(jnp.mean(mine * mine, axis=-1, keepdims=True) + 1e-6)
    normed = (mine * scale * (1.0 + gain_ref[...])).astype(BF16)
    for k in range(2):
        feats[k, dp, own_rows(mp)] = normed[:, k * half : (k + 1) * half]
    spread_mp(lambda m: [feats.at[k, dp, own_rows(m)] for k in range(2)], peers)

    orders = [list(range(1, bits)) + [0], list(range(2, bits)) + [1, 0] if bits > 1 else [0]]
    for t in range(bits):
        waits = []
        for k in range(2):
            bit = orders[k][t]
            peer = flip(dp, bit)
            held = flips(dp, orders[k][:t])
            for i, block in enumerate(held):
                sem = (1 << t) - 1 + i
                copy = remote(
                    feats.at[k, block],
                    feats.at[k, block],
                    ag_send.at[k, sem],
                    ag_recv.at[k, sem],
                    "dp",
                    peer,
                )
                copy.start()
                sends.append(copy)
                other = flip(block, bit)
                waits.append(
                    remote(
                        feats.at[k, other],
                        feats.at[k, other],
                        ag_send.at[k, sem],
                        ag_recv.at[k, sem],
                        "dp",
                        peer,
                    )
                )
        for wait in waits:
            wait.wait_recv()

    for copy in weight_loads[1:]:
        copy.wait()
    all_games = n_dp * games
    units = wg.shape[1]
    tile = math.gcd(units, 256)

    @pl.loop(0, units // tile)
    def _(i):
        columns = pl.ds(pl.multiple_of(i * tile, tile), tile)
        low = feats[0].reshape(all_games, half)
        high = feats[1].reshape(all_games, half)
        gate = dot(low, wg[:half, columns]) + dot(high, wg[half:, columns])
        up = dot(low, wu[:half, columns]) + dot(high, wu[half:, columns])
        bent = jnp.tanh(math.sqrt(2.0 / math.pi) * (gate + 0.044715 * (gate * gate * gate)))
        hidden[:, columns] = (0.5 * gate * (1.0 + bent) * up).astype(BF16)

    def halving(k, t):
        order = orders[k][::-1]
        bit, after = order[t], order[t + 1 :]
        base = sum(1 << (bits - 1 - s) for s in range(t))
        peer = flip(dp, bit)
        waits = []
        for i in range(1 << len(after)):
            keep = with_bits(dp, after, i)
            copy = remote(
                part.at[k, flip(keep, bit)],
                got.at[k, base + i],
                rs_send.at[k, base + i],
                rs_recv.at[k, base + i],
                "dp",
                peer,
            )
            copy.start()
            sends.append(copy)
            waits.append((copy, keep, base + i))
        return waits

    out_tile = math.gcd(half, 512)
    waiting = []
    for k in range(2):

        @pl.loop(0, half // out_tile)
        def _(i):
            columns = pl.ds(pl.multiple_of(k * half + i * out_tile, out_tile), out_tile)
            inner = pl.ds(pl.multiple_of(i * out_tile, out_tile), out_tile)
            block = dot(hidden[...], wd[:, columns]).astype(BF16)
            part[k, :, :, inner] = block.reshape(n_dp, games, out_tile)

        waiting.append(halving(k, 0))
    for t in range(bits):
        later = []
        for k in range(2):
            for copy, keep, slot in waiting[k]:
                copy.wait_recv()
                added = part[k, keep].astype(F32) + got[k, slot].astype(F32)
                if t == bits - 1:
                    head32[:, k * half : (k + 1) * half] = added
                    sums16[:, k * half : (k + 1) * half] = added.astype(BF16)
                else:
                    part[k, keep] = added.astype(BF16)
            if t < bits - 1:
                later.append(halving(k, t + 1))
        waiting = later

    mixed = sum_mp(sums16, sums_got, 3 * peers)
    out_ref[own_rows(mp)] = (mine + mixed).astype(BF16)
    spread_mp(lambda m: [out_ref.at[own_rows(m)]], 4 * peers)
    for copy in sends:
        copy.wait_send()
    arrived_copy.wait()


def local(
    page_pool,
    move_count,
    send_slots,
    page_table,
    history_len,
    queries,
    new_entry,
    residual,
    out_proj,
    ffn_gain,
    gate_proj,
    up_proj,
    down_proj,
):
    n_dp = lax.axis_size("dp")
    n_mp = lax.axis_size("mp")
    pool, page_len, width = page_pool.shape
    cap = send_slots.shape[1]
    games, heads, head_size = queries.shape
    model = residual.shape[1]
    units = gate_proj.shape[1]
    half = model // 2
    share = games // n_mp
    group = math.gcd(pool, n_dp * cap, 8)
    query_rows = jnp.transpose(queries, (1, 0, 2)).reshape(heads * games, head_size)
    vmem = pl.BlockSpec(memory_space=pltpu.VMEM)
    smem = pl.BlockSpec(memory_space=pltpu.SMEM)
    hbm = pl.BlockSpec(memory_space=pl.ANY)
    dma = pltpu.SemaphoreType.DMA
    z_count = 5 * (n_mp - 1)
    return pl.pallas_call(
        functools.partial(step, n_dp, n_mp),
        out_shape=(
            jax.ShapeDtypeStruct((n_dp * cap, page_len, width), BF16),
            jax.ShapeDtypeStruct((games, model), BF16),
        ),
        in_specs=[smem, smem] + [vmem] * 6 + [hbm] * 5,
        out_specs=(hbm, vmem),
        scratch_shapes=[
            pltpu.VMEM((pool, page_len, width), BF16),
            pltpu.VMEM((n_dp * cap, page_len, width), BF16),
            pltpu.VMEM((n_dp * cap, page_len, width), BF16),
            pltpu.VMEM(out_proj.shape, BF16),
            pltpu.VMEM(gate_proj.shape, BF16),
            pltpu.VMEM(up_proj.shape, BF16),
            pltpu.VMEM(down_proj.shape, BF16),
            pltpu.VMEM((games, model), F32),
            pltpu.VMEM((games, model), BF16),
            pltpu.VMEM((games, model), BF16),
            pltpu.VMEM((n_mp - 1, share, model), BF16),
            pltpu.VMEM((n_mp - 1, share, model), BF16),
            pltpu.VMEM((2, n_dp, games, half), BF16),
            pltpu.VMEM((n_dp * games, units), BF16),
            pltpu.VMEM((2, n_dp, games, half), BF16),
            pltpu.VMEM((2, n_dp - 1, games, half), BF16),
            dma((pool // group,)),
            dma((4,)),
            dma,
            dma((n_dp - 1,)),
            dma((n_dp - 1,)),
            dma((z_count,)),
            dma((z_count,)),
            dma((2, n_dp - 1)),
            dma((2, n_dp - 1)),
            dma((2, n_dp - 1)),
            dma((2, n_dp - 1)),
        ],
        compiler_params=pltpu.CompilerParams(
            collective_id=0, has_side_effects=True, vmem_limit_bytes=63 * 1024 * 1024
        ),
        cost_estimate=pl.CostEstimate(
            flops=6 * n_dp * games * model * units,
            bytes_accessed=2 * (page_pool.size + 4 * model * units),
            transcendentals=n_dp * games * units,
        ),
    )(
        move_count,
        send_slots,
        page_table,
        history_len.reshape(games, 1),
        query_rows,
        new_entry,
        residual,
        ffn_gain.reshape(1, model),
        page_pool,
        out_proj,
        gate_proj,
        up_proj,
        down_proj,
    )


def solution(mesh):
    in_specs = (
        P("dp", None, None),
        P("dp", None),
        P("dp", None),
        P("dp", None),
        P("dp"),
        P("dp", "mp", None),
        P("dp", None),
        P("dp", None),
        P("mp", None),
        P(),
        P(None, ("dp", "mp")),
        P(None, ("dp", "mp")),
        P(("dp", "mp"), None),
    )
    out_specs = (P("dp", None, None), P("dp", None))
    return jax.shard_map(local, mesh=mesh, in_specs=in_specs, out_specs=out_specs, check_vma=False)
```

time: 448 us -> 99.4 us (0.22)
  waiting for transfers between devices: 184 us -> 0 us
  local copies, waits for them, and re-layouts: 114 us -> 9.4 us
  matrix products: 104 us -> 0 us
  Pallas kernels: 0 us -> 87.6 us
  other arithmetic: 24.3 us -> 0 us
  between operations: 13.9 us -> 0.65 us
  starting transfers between devices: 4.61 us -> 0 us
    dot_general x27 -> x0, matrix products: 104 us -> none  [the longest x8 46 us: attend_block(): jnp.einsum('bhd,btd->bht', query_blk, keys, preferred_element_type=jnp.fl...]
    gather x9 -> x0, local copies, waits for them, and re-layouts: 104 us -> none  [the longest x8 98.3 us: one_block(): every_page[table_blk].reshape(block, table_len * page_len, width)]
    pallas_call x0 -> x1, Pallas kernels: none -> 87.6 us  [local(): pl.pallas_call(functools.partial(step, n_dp, n_mp), out_shape=(jax.ShapeD...]
    psum x2 -> x0, waiting for transfers between devices: 80 us -> none  [the longest x1 40.7 us: local(): mixed = lax.psum(partial_out, 'mp')]
    reduce_scatter x1 -> x0, waiting for transfers between devices: 51.4 us -> none  [local(): lax.psum_scatter(jnp.dot(hidden, down_proj, preferred_element_type=jnp.fl...]
    all_gather x1 -> x0, waiting for transfers between devices: 28 us -> none  [local(): piece = lax.all_gather(normed, 'dp', axis=0, tiled=True)]
    all_to_all x1 -> x0, waiting for transfers between devices: 24.9 us -> none  [local(): lax.all_to_all(outgoing, 'dp', split_axis=0, concat_axis=0, tiled=True)]
    concatenate x1 -> x0, other arithmetic: 11.4 us -> none  [local(): every_page = jnp.concatenate([page_pool, arrived], axis=0)]
  transfers between devices with their start and end apart: 5 -> 0, of which waited for: 5 -> 0; matrix products, arithmetic and copies ran while one was open for 0% -> 0% of each run, Pallas kernels for 0% -> 0%
where the time goes in v1:
time: 99.4 us; the launch traced here: 97.7 us
  Pallas kernels  87.6 us (88%)
  local copies, waits for them, and re-layouts  9.4 us (9%)
    pallas_call x1, Pallas kernels, local(): pl.pallas_call(functools.partial(step, n_dp, n_mp), out_shape=(jax.ShapeD...  87.6 us
    unnamed x6, local copies, waits for them, and re-layouts  6.57 us

profile of v1, /device:TPU:2, one launch (start us, length us, event | category | flops | bytes accessed | tf_op | source)
XLA Modules:
  0.0 97.7 jit_solution(17767116484775308145)
XLA Ops:
  0.6 1.3 %copy.16.slot_ref = s32[8,2]{1,0:T(8,128)} copy(s32[8,2]{0,1:T(2,128)} %param.15) | data formatting | bytes 128 | tf_op args[2]
  2.0 1.4 %copy.17.table_ref = s32[64,16]{1,0:T(8,128)} copy(s32[64,16]{0,1:T(8,128)} %param.16) | data formatting | bytes 8192 | tf_op args[3]
  3.4 1.4 %copy.18.length_ref = s32[64,1]{1,0:T(8,128)} copy(s32[64,1]{0,1:T(1,128)} %bitcast.7) | data formatting | bytes 512 | tf_op jit(solution)/shard_map/reshape | solution.py:464
  4.7 1.5 %copy.15 = bf16[2,64,256]{2,1,0:T(8,128)(2,1)} copy(bf16[2,64,256]{2,0,1:T(2,128)(2,1)} %bitcast.5) | data formatting | bytes 131072 | tf_op jit(solution)/shard_map/transpose | solution.py:409
  6.2 87.6 %shard_map.140 = (bf16[16,128,512]{2,1,0:T(8,128)(2,1)}, bf16[64,2048]{1,0:T(8,128)(2,1)}) custom-call(s32[1,8]{1,0:T(1,128)} %count_ref.1, s32[8,2]{1,0:T(8,128)} %copy.16.slot_ref, s32[64,16]{1,0:T(8,128)} %copy.17.table_ref, s32[64,1]{1,0:T(8,128)} %copy.18.length_ref, bf16[128,256]{1,0:T(8,128)(2,1)} %bitcast.4, bf16[64,512]{1,0:T(8,128)(2,1)} %entry_ref.1, ...), custom_call_target="tpu_custom_call" | custom-call | flops 3221225472 | bytes 16777216 | tf_op jit(solution)/shard_map/pallas_call | solution.py:415
  93.8 0.0 copy-start
  93.8 3.1 %copy.21 = bf16[16,128,512]{2,1,0:T(8,128)(2,1)} copy(bf16[16,128,512]{2,1,0:T(8,128)(2,1)} %get-tuple-element.4) | data formatting | bytes 4194304
  97.0 0.0 copy-done
  97.0 0.7 copy.22
Async XLA Ops:
  93.8 3.1 %copy-start = (bf16[64,2048]{1,0:T(8,128)(2,1)S(1)}, bf16[64,2048]{1,0:T(8,128)(2,1)}, u32[]{:S(2)}) copy-start(bf16[64,2048]{1,0:T(8,128)(2,1)} %get-tuple-element.5) | copy-start | bytes 786436

commit v2 on v1

--- a/solution.py
+++ b/solution.py
@@ -33,6 +33,13 @@
     for bit in bits:
         found = found + [flip(f, bit) for f in found]
     return found
+
+
+def xor(index, number):
+    for bit in range(number.bit_length()):
+        if (number >> bit) & 1:
+            index = flip(index, bit)
+    return index
 
 
 def with_bits(index, bits, number):
@@ -96,10 +103,10 @@
     mp = lax.axis_index("mp")
     bits = n_dp.bit_length() - 1
     pool, page_len, width = pool_hbm.shape
-    cap = slot_ref.shape[1]
-    games, table_len = table_ref.shape
-    rows, head_size = query_ref.shape
-    heads = rows // games
+    cap = slot_ref.shape[0]
+    table_len, games = table_ref.shape
+    _, heads, head_size = query_ref.shape
+    rows = heads * games
     model = residual_ref.shape[1]
     half = model // 2
     share = games // n_mp
@@ -112,12 +119,6 @@
         )
         copy.start()
         pool_loads.append(copy)
-    weight_loads = []
-    for i, (src, dst) in enumerate(((wo_hbm, wo), (wg_hbm, wg), (wu_hbm, wu), (wd_hbm, wd))):
-        copy = pltpu.make_async_copy(src, dst, weight_sem.at[i])
-        copy.start()
-        weight_loads.append(copy)
-
     barrier = pltpu.get_barrier_semaphore()
     for axis, n, me in (("dp", n_dp, dp), ("mp", n_mp, mp)):
         for o in range(1, n):
@@ -127,34 +128,20 @@
                 device_id={axis: lax.rem(me + o, n)},
                 device_id_type=pl.DeviceIdType.MESH,
             )
-    for copy in pool_loads:
-        copy.wait()
-    for d in range(n_dp):
-        for c in range(cap):
-            page = pages[slot_ref[d, c]]
-            live = jnp.full(page.shape, c < count_ref[0, d])
-            outgoing[d * cap + c] = jnp.where(live, page, jnp.zeros_like(page))
-    pl.semaphore_wait(barrier, n_dp - 1 + n_mp - 1)
-
-    sends = []
-    for o in range(1, n_dp):
-        to = lax.rem(dp + o, n_dp)
-        copy = remote(
-            outgoing.at[pl.ds(to * cap, cap)],
-            landed.at[pl.ds(dp * cap, cap)],
-            page_send.at[o - 1],
-            page_recv.at[o - 1],
-            "dp",
-            to,
-        )
-        copy.start()
-        sends.append(copy)
-    landed[pl.ds(dp * cap, cap)] = outgoing[pl.ds(dp * cap, cap)]
-
-    table = table_ref[...]
     length = length_ref[...]
-    whole_pages = lax.div(length, jnp.int32(page_len))
-    rest = length - whole_pages * page_len
+    whole_row = lax.div(length, jnp.int32(page_len))
+    lines = jnp.concatenate([table_ref[...], whole_row, length - whole_row * page_len], axis=0)
+    down = lax.broadcasted_iota(jnp.int32, (games, games), 0)
+    across = lax.broadcasted_iota(jnp.int32, (games, games), 1)
+    unit = jnp.where(down == across, 1.0, 0.0).astype(BF16)
+    table = lax.dot_general(
+        unit,
+        lines.astype(F32).astype(BF16),
+        (((1,), (1,)), ((), ())),
+        preferred_element_type=F32,
+    ).astype(jnp.int32)
+    whole_pages = table[:, table_len : table_len + 1]
+    rest = table[:, table_len + 1 : table_len + 2]
     lane = lax.broadcasted_iota(jnp.int32, (games, every), 1)
     full = jnp.zeros((games, every), F32)
     last = jnp.full((games, 1), -1, jnp.int32)
@@ -169,7 +156,7 @@
     in_last = jnp.where(place < rest, 1.0, 0.0)
 
     factor = 1.0 / math.sqrt(head_size)
-    query = query_ref[...]
+    query = jnp.concatenate([query_ref[:, h, :] for h in range(heads)], axis=0)
     entry = entry_ref[...].astype(F32)
     entry = jnp.concatenate([entry] * heads, axis=0)
     biggest = (
@@ -177,6 +164,38 @@
     )
     total = jnp.ones((rows, 1), F32)
     acc = entry[:, head_size:]
+
+    for copy in pool_loads:
+        copy.wait()
+    pl.semaphore_wait(barrier, n_dp - 1 + n_mp - 1)
+
+    def picked(d, c):
+        page = pages[slot_ref[c, d]]
+        live = jnp.full(page.shape, c < count_ref[0, d])
+        return jnp.where(live, page, jnp.zeros_like(page))
+
+    sends = []
+    for o in range(n_dp - 1, 0, -1):
+        to = xor(dp, o)
+        for c in range(cap):
+            outgoing[to * cap + c] = picked(to, c)
+        copy = remote(
+            outgoing.at[pl.ds(to * cap, cap)],
+            landed.at[pl.ds(dp * cap, cap)],
+            page_send.at[o - 1],
+            page_recv.at[o - 1],
+            "dp",
+            to,
+        )
+        copy.start()
+        sends.append(copy)
+    for c in range(cap):
+        landed[dp * cap + c] = picked(dp, c)
+    weight_loads = []
+    for i, (src, dst) in enumerate(((wo_hbm, wo), (wg_hbm, wg), (wu_hbm, wu), (wd_hbm, wd))):
+        copy = pltpu.make_async_copy(src, dst, weight_sem.at[i])
+        copy.start()
+        weight_loads.append(copy)
 
     def attend(at, state):
         biggest, total, acc = state
@@ -206,7 +225,7 @@
     for at in range(0, pool, group):
         state = attend(at, state)
     for o in range(1, n_dp):
-        source = lax.rem(dp - o + n_dp, n_dp)
+        source = xor(dp, o)
         slot = landed.at[pl.ds(source * cap, cap)]
         remote(slot, slot, page_send.at[o - 1], page_recv.at[o - 1], "dp", source).wait_recv()
     arrived_copy = pltpu.make_async_copy(landed, arrived_hbm, arrived_sem)
@@ -265,6 +284,9 @@
                 sem = base + (o - 1) * per + i
                 remote(view, view, z_send.at[sem], z_recv.at[sem], "mp", source).wait_recv()
 
+    def place_of(block):
+        return (block % 2) * (n_dp // 2) + block // 2
+
     def own_rows(m):
         return pl.ds(pl.multiple_of(m * share, share), share)
 
@@ -273,8 +295,8 @@
     scale = lax.rsqrt(jnp.mean(mine * mine, axis=-1, keepdims=True) + 1e-6)
     normed = (mine * scale * (1.0 + gain_ref[...])).astype(BF16)
     for k in range(2):
-        feats[k, dp, own_rows(mp)] = normed[:, k * half : (k + 1) * half]
-    spread_mp(lambda m: [feats.at[k, dp, own_rows(m)] for k in range(2)], peers)
+        feats[k, place_of(dp), own_rows(mp)] = normed[:, k * half : (k + 1) * half]
+    spread_mp(lambda m: [feats.at[k, place_of(dp), own_rows(m)] for k in range(2)], peers)
 
     orders = [list(range(1, bits)) + [0], list(range(2, bits)) + [1, 0] if bits > 1 else [0]]
     for t in range(bits):
@@ -286,8 +308,8 @@
             for i, block in enumerate(held):
                 sem = (1 << t) - 1 + i
                 copy = remote(
-                    feats.at[k, block],
-                    feats.at[k, block],
+                    feats.at[k, place_of(block)],
+                    feats.at[k, place_of(block)],
                     ag_send.at[k, sem],
                     ag_recv.at[k, sem],
                     "dp",
@@ -298,32 +320,44 @@
                 other = flip(block, bit)
                 waits.append(
                     remote(
-                        feats.at[k, other],
-                        feats.at[k, other],
+                        feats.at[k, place_of(other)],
+                        feats.at[k, place_of(other)],
                         ag_send.at[k, sem],
                         ag_recv.at[k, sem],
                         "dp",
                         peer,
                     )
                 )
-        for wait in waits:
-            wait.wait_recv()
+        if t < bits - 1:
+            for wait in waits:
+                wait.wait_recv()
+
+    near = dp % 2
+    blocks = n_dp // 2
+    some_games = blocks * games
+    units = wg.shape[1]
+    tile = math.gcd(units, 256)
+
+    def rows_of(side):
+        return pl.ds(pl.multiple_of(side * some_games, some_games), some_games)
+
+    def expand(side):
+        @pl.loop(0, units // tile)
+        def _(i):
+            columns = pl.ds(pl.multiple_of(i * tile, tile), tile)
+            low = feats[0, pl.ds(side * blocks, blocks)].reshape(some_games, half)
+            high = feats[1, pl.ds(side * blocks, blocks)].reshape(some_games, half)
+            gate = dot(low, wg[:half, columns]) + dot(high, wg[half:, columns])
+            up = dot(low, wu[:half, columns]) + dot(high, wu[half:, columns])
+            bent = jnp.tanh(math.sqrt(2.0 / math.pi) * (gate + 0.044715 * (gate * gate * gate)))
+            hidden[rows_of(side), columns] = (0.5 * gate * (1.0 + bent) * up).astype(BF16)
 
     for copy in weight_loads[1:]:
         copy.wait()
-    all_games = n_dp * games
-    units = wg.shape[1]
-    tile = math.gcd(units, 256)
-
-    @pl.loop(0, units // tile)
-    def _(i):
-        columns = pl.ds(pl.multiple_of(i * tile, tile), tile)
-        low = feats[0].reshape(all_games, half)
-        high = feats[1].reshape(all_games, half)
-        gate = dot(low, wg[:half, columns]) + dot(high, wg[half:, columns])
-        up = dot(low, wu[:half, columns]) + dot(high, wu[half:, columns])
-        bent = jnp.tanh(math.sqrt(2.0 / math.pi) * (gate + 0.044715 * (gate * gate * gate)))
-        hidden[:, columns] = (0.5 * gate * (1.0 + bent) * up).astype(BF16)
+    expand(near)
+    for wait in waits:
+        wait.wait_recv()
+    expand(1 - near)
 
     def halving(k, t):
         order = orders[k][::-1]
@@ -334,7 +368,7 @@
         for i in range(1 << len(after)):
             keep = with_bits(dp, after, i)
             copy = remote(
-                part.at[k, flip(keep, bit)],
+                part.at[k, place_of(flip(keep, bit))],
                 got.at[k, base + i],
                 rs_send.at[k, base + i],
                 rs_recv.at[k, base + i],
@@ -347,28 +381,32 @@
         return waits
 
     out_tile = math.gcd(half, 512)
-    waiting = []
-    for k in range(2):
-
+
+    def project(side, k):
         @pl.loop(0, half // out_tile)
         def _(i):
             columns = pl.ds(pl.multiple_of(k * half + i * out_tile, out_tile), out_tile)
             inner = pl.ds(pl.multiple_of(i * out_tile, out_tile), out_tile)
-            block = dot(hidden[...], wd[:, columns]).astype(BF16)
-            part[k, :, :, inner] = block.reshape(n_dp, games, out_tile)
-
+            block = dot(hidden[rows_of(side)], wd[:, columns]).astype(BF16)
+            part[k, pl.ds(side * blocks, blocks), :, inner] = block.reshape(blocks, games, out_tile)
+
+    waiting = []
+    for k in range(2):
+        project(1 - near, k)
         waiting.append(halving(k, 0))
+    for k in range(2):
+        project(near, k)
     for t in range(bits):
         later = []
         for k in range(2):
             for copy, keep, slot in waiting[k]:
                 copy.wait_recv()
-                added = part[k, keep].astype(F32) + got[k, slot].astype(F32)
+                added = part[k, place_of(keep)].astype(F32) + got[k, slot].astype(F32)
                 if t == bits - 1:
                     head32[:, k * half : (k + 1) * half] = added
                     sums16[:, k * half : (k + 1) * half] = added.astype(BF16)
                 else:
-                    part[k, keep] = added.astype(BF16)
+                    part[k, place_of(keep)] = added.astype(BF16)
             if t < bits - 1:
                 later.append(halving(k, t + 1))
         waiting = later
@@ -406,7 +444,6 @@
     half = model // 2
     share = games // n_mp
     group = math.gcd(pool, n_dp * cap, 8)
-    query_rows = jnp.transpose(queries, (1, 0, 2)).reshape(heads * games, head_size)
     vmem = pl.BlockSpec(memory_space=pltpu.VMEM)
     smem = pl.BlockSpec(memory_space=pltpu.SMEM)
     hbm = pl.BlockSpec(memory_space=pl.ANY)
@@ -459,10 +496,10 @@
         ),
     )(
         move_count,
-        send_slots,
-        page_table,
-        history_len.reshape(games, 1),
-        query_rows,
+        send_slots.T,
+        page_table.T,
+        history_len.reshape(1, games),
+        queries,
         new_entry,
         residual,
         ffn_gain.reshape(1, model),

time: 99.4 us -> 97.8 us (0.984); the launches traced: 97.7 us -> 97.6 us
  local copies, waits for them, and re-layouts: 9.4 us -> 3.84 us
  Pallas kernels: 87.6 us -> 93.1 us
    pallas_call x1, Pallas kernels: 87.6 us -> 93.1 us  [local(): pl.pallas_call(functools.partial(step, n_dp, n_mp), out_shape=(jax.ShapeD...]
    unnamed x6 -> x4, local copies, waits for them, and re-layouts: 6.57 us -> 3.84 us
    transpose x1 -> x0, local copies, waits for them, and re-layouts: 1.48 us -> none  [local(): jnp.transpose(queries, (1, 0, 2)).reshape(heads * games, head_size)]
    reshape x1 -> x0, local copies, waits for them, and re-layouts: 1.35 us -> none  [local(): history_len.reshape(games, 1)]
where the time goes in v2:
time: 97.8 us; the launch traced here: 97.6 us
  Pallas kernels  93.1 us (95%)
  local copies, waits for them, and re-layouts  3.84 us (4%)
    pallas_call x1, Pallas kernels, local(): pl.pallas_call(functools.partial(step, n_dp, n_mp), out_shape=(jax.ShapeD...  93.1 us
    unnamed x4, local copies, waits for them, and re-layouts  3.84 us

profile of v2, /device:TPU:2, one launch (start us, length us, event | category | flops | bytes accessed | tf_op | source)
XLA Modules:
  0.0 97.6 jit_solution(10046200916476869516)
XLA Ops:
  0.6 93.1 %shard_map.140 = (bf16[16,128,512]{2,1,0:T(8,128)(2,1)}, bf16[64,2048]{1,0:T(8,128)(2,1)}) custom-call(s32[1,8]{1,0:T(1,128)} %count_ref.1, s32[2,8]{1,0:T(2,128)} %bitcast.6, s32[16,64]{1,0:T(8,128)} %bitcast.4, s32[1,64]{1,0:T(1,128)} %bitcast.7, bf16[64,2,256]{2,1,0:T(2,128)(2,1)} %query_ref.1, bf16[64,512]{1,0:T(8,128)(2,1)} %entry_ref.1, ...), custom_call_target="tpu_custom_call" | custom-call | flops 3221225472 | bytes 16777216 | tf_op jit(solution)/shard_map/pallas_call | solution.py:452
  93.7 0.0 copy-start
  93.8 3.1 %copy.17 = bf16[16,128,512]{2,1,0:T(8,128)(2,1)} copy(bf16[16,128,512]{2,1,0:T(8,128)(2,1)} %get-tuple-element.4) | data formatting | bytes 4194304
  96.9 0.0 copy-done
  96.9 0.7 copy.18
Async XLA Ops:
  93.7 3.1 %copy-start = (bf16[64,2048]{1,0:T(8,128)(2,1)S(1)}, bf16[64,2048]{1,0:T(8,128)(2,1)}, u32[]{:S(2)}) copy-start(bf16[64,2048]{1,0:T(8,128)(2,1)} %get-tuple-element.5) | copy-start | bytes 786436
